TPU v7x, 32 devices: a whole 2x2x4 slice. The times are simulated.
32 devices in a mesh: gx: 2 (over core), gy: 4 (over y, x), gz: 4 (over z).
Axes of the slice: x: 2, y: 2, z: 4, core: 2. Of those that a mesh axis runs over, the one named last changes fastest.
Arguments:
- dual_matrix: float32 [2, 4, 4, 1536, 1536], P('gx', 'gy', 'gz'), may hold values from -1 to 4, as said below
- modes: float32 [2, 4, 4, 6, 1536], P('gx', 'gy', 'gz'), may hold values from -0.15625 to 0.15625
- coarse_rows: float32 [192, 192], P(('gx', 'gy', 'gz')), may hold values from -0.2 to 0.4, as said below
- loads: float32 [2, 4, 4, 8, 6, 128], P('gx', 'gy', 'gz'), may hold values from -40 to 40
- face_counts: int32 [2, 4, 4, 3], replicated, may hold values from 32 to 128
- contact: int32 [2, 4, 4, 6, 128], P('gx', 'gy', 'gz'), may hold values 0 or 1
Outputs:
- multipliers: float32 [2, 4, 4, 8, 6, 128], P('gx', 'gy', 'gz')
- residual: float32 [2, 4, 4, 8, 6, 128], P('gx', 'gy', 'gz')
Inputs may be any that keep to these rules, and one draw needn't show every extreme that they name: `dual_matrix`: every subdomain's matrix is symmetric positive definite. `coarse_rows`: the coarse operator is symmetric positive definite.
All inputs are finite; a program needn't handle non-finite values. No bound on the sum of `contact` on one device may be relied on, other than what follows from the above.
Results may differ from a plain program's by a relative error of at most 0.0003.
Values sent between devices are 32-bit elements; how exact they have to be, the bound alone decides.
A program may use at most 128 MiB of HBM per device.

v0:
```python
import jax
import jax.numpy as jnp
from jax import lax
from jax.sharding import PartitionSpec as P

ITERS = 4
highest = lax.Precision.HIGHEST


def from_behind(block, axis, distance):
    devices = range(lax.axis_size(axis))
    route = [((i - distance) % len(devices), i) for i in devices]
    return lax.ppermute(block, axis, route)


def trade(upper_faces, lower_faces):
    from_below = [
        from_behind(upper_faces[0], "gx", 1),
        from_behind(upper_faces[1], "gy", 1),
        from_behind(upper_faces[2], "gz", 1),
    ]
    from_above = [
        from_behind(lower_faces[0], "gx", -1),
        from_behind(lower_faces[1], "gy", -1),
        from_behind(lower_faces[2], "gz", -1),
    ]
    return (from_below, from_above)


def spread_faces(owned_vec):
    upper_faces = [owned_vec[..., 2 * grid_axis + 1, :] for grid_axis in range(3)]
    lower_faces = [owned_vec[..., 2 * grid_axis, :] for grid_axis in range(3)]
    from_below, from_above = trade(upper_faces, lower_faces)
    faces = []
    for grid_axis in range(3):
        faces.append(jnp.concatenate([from_below[grid_axis], lower_faces[grid_axis]], axis=-1))
        faces.append(jnp.concatenate([upper_faces[grid_axis], from_above[grid_axis]], axis=-1))
    return jnp.stack(faces, axis=-2)


def collect_faces(local_form):
    half_width = local_form.shape[-1] // 2
    upper_faces = [local_form[..., 2 * grid_axis + 1, half_width:] for grid_axis in range(3)]
    lower_faces = [local_form[..., 2 * grid_axis, :half_width] for grid_axis in range(3)]
    from_below, from_above = trade(upper_faces, lower_faces)
    pieces = []
    for grid_axis in range(3):
        pieces.append(local_form[..., 2 * grid_axis, half_width:] + from_below[grid_axis])
        pieces.append(local_form[..., 2 * grid_axis + 1, :half_width] + from_above[grid_axis])
    return jnp.stack(pieces, axis=-2)


def coarse_weights(flattened, own_modes, coarse_rows):
    on_modes = jnp.einsum("jm,km->jk", own_modes, flattened, precision=highest)
    return jnp.dot(
        coarse_rows,
        lax.all_gather(on_modes, ("gx", "gy", "gz"), axis=0, tiled=True),
        precision=highest,
    )


def on_device(dual_matrix, modes, coarse_rows, loads, face_counts, contact):
    half_width = loads.shape[-1]
    case_count = loads.shape[3]
    grid_pos = [lax.axis_index("gx"), lax.axis_index("gy"), lax.axis_index("gz")]
    grid_sizes = [lax.axis_size("gx"), lax.axis_size("gy"), lax.axis_size("gz")]

    def counts_at(where):
        return lax.dynamic_slice(
            face_counts, (where[0], where[1], where[2], 0), (1, 1, 1, 3)
        ).reshape(3)

    own_counts = counts_at(grid_pos)
    positions = jnp.arange(half_width, dtype=jnp.int32)
    own_masks = []
    local_masks = []
    for grid_axis in range(3):
        lower_pos = list(grid_pos)
        lower_pos[grid_axis] = (grid_pos[grid_axis] - 1 + grid_sizes[grid_axis]) % grid_sizes[
            grid_axis
        ]
        lower_count = counts_at(lower_pos)[grid_axis]
        lower_row = (positions < lower_count).astype(jnp.float32)
        upper_row = (positions < own_counts[grid_axis]).astype(jnp.float32)
        own_masks.extend([lower_row, upper_row])
        local_masks.extend(
            [jnp.concatenate([lower_row, lower_row]), jnp.concatenate([upper_row, upper_row])]
        )
    active_own = jnp.stack(own_masks).reshape(1, 1, 1, 1, 6, half_width)
    is_contact = contact[:, :, :, None] == 1
    matrix = dual_matrix[0, 0, 0]
    own_modes = modes[0, 0, 0]

    def local_coarse(local_form):
        flattened = local_form.reshape(case_count, -1)
        weights = coarse_weights(flattened, own_modes, coarse_rows)
        return jnp.einsum("jk,jm->km", weights, own_modes, precision=highest).reshape(
            local_form.shape
        )

    def project(vector):
        return vector - collect_faces(local_coarse(spread_faces(vector))) * active_own

    start_vector = loads * active_own

    def partial_inner(first, second):
        return jnp.sum(first * second, axis=(0, 1, 2, 4, 5))

    multipliers = jnp.zeros(loads.shape, jnp.float32)
    residual = start_vector

    def energy_sum(first, second):
        return lax.psum(partial_inner(first, second), ("gx", "gy", "gz")).reshape(-1, 1, 1)

    precond = project(residual)
    direction = precond
    energy = energy_sum(residual, precond)
    for rounds in range(ITERS):
        local_local_form = spread_faces(direction)
        local_flattened = local_local_form.reshape(case_count, -1)
        dual_image = (
            collect_faces(
                jnp.dot(local_flattened, matrix, precision=highest).reshape(local_local_form.shape)
            )
            * active_own
        )
        curvature = lax.psum(partial_inner(direction, dual_image), ("gx", "gy", "gz")).reshape(
            -1, 1, 1
        )
        step_size = energy / curvature
        updated = multipliers + step_size * direction
        multipliers = jnp.where(is_contact, jnp.maximum(updated, 0.0), updated)
        residual = residual - step_size * dual_image
        if rounds + 1 < ITERS:
            precond = project(residual)
            energy_next = energy_sum(residual, precond)
            direction = precond + energy_next / energy * direction
            energy = energy_next
    return (multipliers, residual)


def solution(mesh):
    return jax.shard_map(
        on_device,
        mesh=mesh,
        in_specs=(
            P("gx", "gy", "gz", None, None),
            P("gx", "gy", "gz", None, None),
            P(("gx", "gy", "gz"), None),
            P("gx", "gy", "gz", None, None, None),
            P(),
            P("gx", "gy", "gz", None, None),
        ),
        out_specs=(P("gx", "gy", "gz", None, None, None), P("gx", "gy", "gz", None, None, None)),
        check_vma=False,
    )
```

profile of v0, /device:TPU:0, one launch (start us, length us, event | category | flops | bytes accessed | tf_op | source)
XLA Modules:
  0.0 787.7 jit_solution(9719686072488246595)
XLA Ops:
  7.4 2.9 collective-permute-start.2
  18.8 67.1 %all-gather = f32[32,6,8]{2,1,0:T(8,128)S(1)} all-gather(f32[1,6,8]{2,1,0:T(8,128)S(1)} %bitcast.1086), channel_id=1, replica_groups=mesh['gx'=2,'gy'=4,'gz'=4] {'gx','gy','gz'}, dimensions={0}, use_global_device_ids=true | all-gather | bytes 6336 | tf_op jit(solution)/shard_map/all_gather | solution.py:57
  91.9 3.9 collective-permute-start.11
  95.8 4.1 collective-permute-done.9
  100.8 9.6 %copy.36 = f32[1,1,1,1536,1536]{3,4,2,1,0:T(8,128)} copy(f32[1,1,1,1536,1536]{4,3,2,1,0:T(8,128)} %param.6) | data formatting | bytes 18874368 | tf_op args[0]
  110.9 3.8 collective-permute-start.14
  114.7 3.9 collective-permute-start.17
  120.1 10.1 %convolution_bitcast_fusion.6 = f32[1,1,1,8,6,256]{5,3,4,2,1,0:T(8,128)S(1)} fusion(f32[8,1536,1]{1,0,2:T(8,128)S(1)} %bitcast.1078, f32[6,256,1536]{2,1,0:T(8,128)} %bitcast.1070), kind=kOutput, calls=%fused_computation.6 | convolution fusion | flops 226492416 | bytes 9535488 | tf_op jit(solution)/shard_map/dot_general | solution.py:123
  130.8 2.9 collective-permute-start.20
  134.9 2.8 collective-permute-start.23
  139.4 41.9 %all-reduce = (f32[8]{0:T(128)S(1)}, f32[8]{0:T(128)S(1)}) all-reduce(f32[8]{0:T(128)S(1)} %get-tuple-element.3, f32[8]{0:T(128)S(1)} %get-tuple-element.2), channel_id=1, replica_groups=mesh['gx'=2,'gy'=4,'gz'=4] {'gx','gy','gz'}, use_global_device_ids=true, to_apply=%region_1.2 | all-reduce | flops 16 | bytes 128 | tf_op jit(solution)/shard_map/psum | solution.py:113
  191.2 67.3 %all-gather.1 = f32[32,6,8]{2,1,0:T(8,128)S(1)} all-gather(f32[1,6,8]{2,1,0:T(8,128)S(1)} %bitcast.1087), channel_id=1, replica_groups=mesh['gx'=2,'gy'=4,'gz'=4] {'gx','gy','gz'}, dimensions={0}, use_global_device_ids=true | all-gather | bytes 6336 | tf_op jit(solution)/shard_map/all_gather | solution.py:57
  259.1 2.5 collective-permute-start.30
  264.6 3.8 collective-permute-start.35
  268.4 3.6 collective-permute-done.33
  272.2 42.4 %psum.58 = f32[8]{0:T(128)S(1)} all-reduce(f32[8]{0:T(128)S(1)} %multiply_reduce_fusion.5), channel_id=1, replica_groups=mesh['gx'=2,'gy'=4,'gz'=4] {'gx','gy','gz'}, use_global_device_ids=true, to_apply=%region_5.6 | all-reduce | flops 8 | bytes 64 | tf_op jit(solution)/shard_map/psum | solution.py:113
  324.7 10.1 %convolution_bitcast_fusion.4 = f32[1,1,1,8,6,256]{5,3,4,2,1,0:T(8,128)S(1)} fusion(f32[8,1536,1]{1,0,2:T(8,128)S(1)} %bitcast.1079, f32[6,256,1536]{2,1,0:T(8,128)} %bitcast.1071), kind=kOutput, calls=%fused_computation.4 | convolution fusion | flops 226492416 | bytes 9535488 | tf_op jit(solution)/shard_map/dot_general | solution.py:123
  343.8 39.2 %psum.59 = f32[8]{0:T(128)S(1)} all-reduce(f32[8]{0:T(128)S(1)} %multiply_reduce_fusion.4), channel_id=1, replica_groups=mesh['gx'=2,'gy'=4,'gz'=4] {'gx','gy','gz'}, use_global_device_ids=true, to_apply=%region_7.8 | all-reduce | flops 8 | bytes 64 | tf_op jit(solution)/shard_map/psum | solution.py:127
  393.0 66.9 %all-gather.2 = f32[32,6,8]{2,1,0:T(8,128)S(1)} all-gather(f32[1,6,8]{2,1,0:T(8,128)S(1)} %bitcast.1088), channel_id=1, replica_groups=mesh['gx'=2,'gy'=4,'gz'=4] {'gx','gy','gz'}, dimensions={0}, use_global_device_ids=true | all-gather | bytes 6336 | tf_op jit(solution)/shard_map/all_gather | solution.py:57
  460.4 2.5 collective-permute-start.54
  466.0 3.8 collective-permute-start.59
  469.8 4.1 collective-permute-done.57
  474.1 42.4 %psum.60 = f32[8]{0:T(128)S(1)} all-reduce(f32[8]{0:T(128)S(1)} %multiply_reduce_fusion.3), channel_id=1, replica_groups=mesh['gx'=2,'gy'=4,'gz'=4] {'gx','gy','gz'}, use_global_device_ids=true, to_apply=%region_9.10 | all-reduce | flops 8 | bytes 64 | tf_op jit(solution)/shard_map/psum | solution.py:113
  526.6 10.1 %convolution_bitcast_fusion.2 = f32[1,1,1,8,6,256]{5,3,4,2,1,0:T(8,128)S(1)} fusion(f32[8,1536,1]{1,0,2:T(8,128)S(1)} %bitcast.1080, f32[6,256,1536]{2,1,0:T(8,128)} %bitcast.1072), kind=kOutput, calls=%fused_computation.2 | convolution fusion | flops 226492416 | bytes 9535488 | tf_op jit(solution)/shard_map/dot_general | solution.py:123
  545.7 39.2 %psum.61 = f32[8]{0:T(128)S(1)} all-reduce(f32[8]{0:T(128)S(1)} %multiply_reduce_fusion.2), channel_id=1, replica_groups=mesh['gx'=2,'gy'=4,'gz'=4] {'gx','gy','gz'}, use_global_device_ids=true, to_apply=%region_11.12 | all-reduce | flops 8 | bytes 64 | tf_op jit(solution)/shard_map/psum | solution.py:127
  594.9 66.9 %all-gather.3 = f32[32,6,8]{2,1,0:T(8,128)S(1)} all-gather(f32[1,6,8]{2,1,0:T(8,128)S(1)} %bitcast.1089), channel_id=1, replica_groups=mesh['gx'=2,'gy'=4,'gz'=4] {'gx','gy','gz'}, dimensions={0}, use_global_device_ids=true | all-gather | bytes 6336 | tf_op jit(solution)/shard_map/all_gather | solution.py:57
  662.3 2.5 collective-permute-start.78
  667.9 3.8 collective-permute-start.83
  671.7 4.1 collective-permute-done.81
  676.0 42.4 %psum.62 = f32[8]{0:T(128)S(1)} all-reduce(f32[8]{0:T(128)S(1)} %multiply_reduce_fusion.1), channel_id=1, replica_groups=mesh['gx'=2,'gy'=4,'gz'=4] {'gx','gy','gz'}, use_global_device_ids=true, to_apply=%region_13.14 | all-reduce | flops 8 | bytes 64 | tf_op jit(solution)/shard_map/psum | solution.py:113
  728.5 10.1 %convolution_bitcast_fusion = f32[1,1,1,8,6,256]{5,3,4,2,1,0:T(8,128)S(1)} fusion(f32[8,1536,1]{1,0,2:T(8,128)S(1)} %bitcast.1081, f32[6,256,1536]{2,1,0:T(8,128)} %bitcast.1073), kind=kOutput, calls=%fused_computation | convolution fusion | flops 226492416 | bytes 9535488 | tf_op jit(solution)/shard_map/dot_general | solution.py:123
  747.7 39.3 %psum.63 = f32[8]{0:T(128)S(1)} all-reduce(f32[8]{0:T(128)S(1)} %multiply_reduce_fusion), channel_id=1, replica_groups=mesh['gx'=2,'gy'=4,'gz'=4] {'gx','gy','gz'}, use_global_device_ids=true, to_apply=%region_15.16 | all-reduce | flops 8 | bytes 64 | tf_op jit(solution)/shard_map/psum | solution.py:127
  (348 shorter events, 125.9 us)
Async XLA Ops:
  6.9 7.2 collective-permute-start
  7.3 8.9 %collective-permute-start.1 = (f32[1,1,1,8,128]{4,3,2,1,0:T(8,128)S(1)}, f32[1,1,1,8,128]{4,3,2,1,0:T(8,128)S(1)}, u32[]{:S(2)}, u32[]{:S(2)}) collective-permute-start(f32[1,1,1,8,128]{4,3,2,1,0:T(8,128)S(1)} %get-tuple-element.100), channel_id=1, source_target_pairs={{16,0},{0,16},{17,1},{1,17},{18,2},{2,18},{19,3},{3,19},{20,4},{4,... | collective-permute-start | bytes 12296 | tf_op jit(solution)/shard_map/ppermute | solution.py:13
  7.4 8.8 %collective-permute-start.2 = (f32[1,1,1,8,128]{4,3,2,1,0:T(8,128)S(1)}, f32[1,1,1,8,128]{4,3,2,1,0:T(8,128)S(1)}, u32[]{:S(2)}, u32[]{:S(2)}) collective-permute-start(f32[1,1,1,8,128]{4,3,2,1,0:T(8,128)S(1)} %get-tuple-element.99), channel_id=1, source_target_pairs={{12,0},{0,4},{4,8},{8,12},{13,1},{1,5},{5,9},{9,13},{14,2},{2,6},{... | collective-permute-start | bytes 12296 | tf_op jit(solution)/shard_map/ppermute | solution.py:13
  90.6 9.4 %collective-permute-start.9 = (f32[1,1,1,8,128]{4,3,2,1,0:T(8,128)S(1)}, f32[1,1,1,8,128]{4,3,2,1,0:T(8,128)S(1)}, u32[]{:S(2)}, u32[]{:S(2)}) collective-permute-start(f32[1,1,1,8,128]{4,3,2,1,0:T(8,128)S(1)} %get-tuple-element.50), channel_id=1, source_target_pairs={{4,0},{8,4},{12,8},{0,12},{5,1},{9,5},{13,9},{1,13},{6,2},{10,6},{... | collective-permute-start | bytes 12296 | tf_op jit(solution)/shard_map/ppermute | solution.py:13
  91.9 8.0 %collective-permute-start.10 = (f32[1,1,1,8,128]{4,3,2,1,0:T(8,128)S(1)}, f32[1,1,1,8,128]{4,3,2,1,0:T(8,128)S(1)}, u32[]{:S(2)}, u32[]{:S(2)}) collective-permute-start(f32[1,1,1,8,128]{4,3,2,1,0:T(8,128)S(1)} %get-tuple-element.49), channel_id=1, source_target_pairs={{3,0},{0,1},{1,2},{2,3},{7,4},{4,5},{5,6},{6,7},{11,8},{8,9},{9,10... | collective-permute-start | bytes 12296 | tf_op jit(solution)/shard_map/ppermute | solution.py:13
  91.9 8.0 %collective-permute-start.11 = (f32[1,1,1,8,128]{4,3,2,1,0:T(8,128)S(1)}, f32[1,1,1,8,128]{4,3,2,1,0:T(8,128)S(1)}, u32[]{:S(2)}, u32[]{:S(2)}) collective-permute-start(f32[1,1,1,8,128]{4,3,2,1,0:T(8,128)S(1)} %get-tuple-element.48), channel_id=1, source_target_pairs={{1,0},{2,1},{3,2},{0,3},{5,4},{6,5},{7,6},{4,7},{9,8},{10,9},{11,1... | collective-permute-start | bytes 12296 | tf_op jit(solution)/shard_map/ppermute | solution.py:13
  100.7 14.0 %collective-permute-start.12 = (f32[1,1,1,8,128]{4,3,2,1,0:T(8,128)S(1)}, f32[1,1,1,8,128]{4,3,2,1,0:T(8,128)S(1)}, u32[]{:S(2)}, u32[]{:S(2)}) collective-permute-start(f32[1,1,1,8,128]{4,3,2,1,0:T(8,128)S(1)} %get-tuple-element.95), channel_id=1, source_target_pairs={{16,0},{0,16},{17,1},{1,17},{18,2},{2,18},{19,3},{3,19},{20,4},{4,... | collective-permute-start | bytes 12296 | tf_op jit(solution)/shard_map/ppermute | solution.py:13
  110.5 8.1 %collective-permute-start.13 = (f32[1,1,1,8,128]{4,3,2,1,0:T(8,128)S(1)}, f32[1,1,1,8,128]{4,3,2,1,0:T(8,128)S(1)}, u32[]{:S(2)}, u32[]{:S(2)}) collective-permute-start(f32[1,1,1,8,128]{4,3,2,1,0:T(8,128)S(1)} %get-tuple-element.94), channel_id=1, source_target_pairs={{16,0},{0,16},{17,1},{1,17},{18,2},{2,18},{19,3},{3,19},{20,4},{4,... | collective-permute-start | bytes 12296 | tf_op jit(solution)/shard_map/ppermute | solution.py:13
  110.9 7.7 collective-permute-start.14
  130.3 7.4 collective-permute-start.19
  181.4 8.0 %collective-permute-start.25 = (f32[1,1,1,8,128]{4,3,2,1,0:T(8,128)S(1)}, f32[1,1,1,8,128]{4,3,2,1,0:T(8,128)S(1)}, u32[]{:S(2)}, u32[]{:S(2)}) collective-permute-start(f32[1,1,1,8,128]{4,3,2,1,0:T(8,128)S(1)} %get-tuple-element.88), channel_id=1, source_target_pairs={{16,0},{0,16},{17,1},{1,17},{18,2},{2,18},{19,3},{3,19},{20,4},{4,... | collective-permute-start | bytes 12296 | tf_op jit(solution)/shard_map/ppermute | solution.py:13
  181.9 7.5 collective-permute-start.26
  262.7 9.4 %collective-permute-start.33 = (f32[1,1,1,8,128]{4,3,2,1,0:T(8,128)S(1)}, f32[1,1,1,8,128]{4,3,2,1,0:T(8,128)S(1)}, u32[]{:S(2)}, u32[]{:S(2)}) collective-permute-start(f32[1,1,1,8,128]{4,3,2,1,0:T(8,128)S(1)} %get-tuple-element.38), channel_id=1, source_target_pairs={{4,0},{8,4},{12,8},{0,12},{5,1},{9,5},{13,9},{1,13},{6,2},{10,6},{... | collective-permute-start | bytes 12296 | tf_op jit(solution)/shard_map/ppermute | solution.py:13
  264.6 7.5 collective-permute-start.34
  264.6 7.5 collective-permute-start.35
  314.7 8.1 %collective-permute-start.37 = (f32[1,1,1,8,128]{4,3,2,1,0:T(8,128)S(1)}, f32[1,1,1,8,128]{4,3,2,1,0:T(8,128)S(1)}, u32[]{:S(2)}, u32[]{:S(2)}) collective-permute-start(f32[1,1,1,8,128]{4,3,2,1,0:T(8,128)S(1)} %get-tuple-element.82), channel_id=1, source_target_pairs={{16,0},{0,16},{17,1},{1,17},{18,2},{2,18},{19,3},{3,19},{20,4},{4,... | collective-permute-start | bytes 12296 | tf_op jit(solution)/shard_map/ppermute | solution.py:13
  315.2 7.6 collective-permute-start.38
  334.9 7.3 collective-permute-start.43
  383.2 7.5 collective-permute-start.49
  464.5 9.4 %collective-permute-start.57 = (f32[1,1,1,8,128]{4,3,2,1,0:T(8,128)S(1)}, f32[1,1,1,8,128]{4,3,2,1,0:T(8,128)S(1)}, u32[]{:S(2)}, u32[]{:S(2)}) collective-permute-start(f32[1,1,1,8,128]{4,3,2,1,0:T(8,128)S(1)} %get-tuple-element.26), channel_id=1, source_target_pairs={{4,0},{8,4},{12,8},{0,12},{5,1},{9,5},{13,9},{1,13},{6,2},{10,6},{... | collective-permute-start | bytes 12296 | tf_op jit(solution)/shard_map/ppermute | solution.py:13
  466.0 8.0 %collective-permute-start.58 = (f32[1,1,1,8,128]{4,3,2,1,0:T(8,128)S(1)}, f32[1,1,1,8,128]{4,3,2,1,0:T(8,128)S(1)}, u32[]{:S(2)}, u32[]{:S(2)}) collective-permute-start(f32[1,1,1,8,128]{4,3,2,1,0:T(8,128)S(1)} %get-tuple-element.25), channel_id=1, source_target_pairs={{3,0},{0,1},{1,2},{2,3},{7,4},{4,5},{5,6},{6,7},{11,8},{8,9},{9,10... | collective-permute-start | bytes 12296 | tf_op jit(solution)/shard_map/ppermute | solution.py:13
  466.0 8.0 %collective-permute-start.59 = (f32[1,1,1,8,128]{4,3,2,1,0:T(8,128)S(1)}, f32[1,1,1,8,128]{4,3,2,1,0:T(8,128)S(1)}, u32[]{:S(2)}, u32[]{:S(2)}) collective-permute-start(f32[1,1,1,8,128]{4,3,2,1,0:T(8,128)S(1)} %get-tuple-element.24), channel_id=1, source_target_pairs={{1,0},{2,1},{3,2},{0,3},{5,4},{6,5},{7,6},{4,7},{9,8},{10,9},{11,1... | collective-permute-start | bytes 12296 | tf_op jit(solution)/shard_map/ppermute | solution.py:13
  516.6 8.1 %collective-permute-start.61 = (f32[1,1,1,8,128]{4,3,2,1,0:T(8,128)S(1)}, f32[1,1,1,8,128]{4,3,2,1,0:T(8,128)S(1)}, u32[]{:S(2)}, u32[]{:S(2)}) collective-permute-start(f32[1,1,1,8,128]{4,3,2,1,0:T(8,128)S(1)} %get-tuple-element.70), channel_id=1, source_target_pairs={{16,0},{0,16},{17,1},{1,17},{18,2},{2,18},{19,3},{3,19},{20,4},{4,... | collective-permute-start | bytes 12296 | tf_op jit(solution)/shard_map/ppermute | solution.py:13
  517.1 7.6 collective-permute-start.62
  536.8 7.3 collective-permute-start.67
  585.1 7.5 collective-permute-start.73
  666.4 9.4 %collective-permute-start.81 = (f32[1,1,1,8,128]{4,3,2,1,0:T(8,128)S(1)}, f32[1,1,1,8,128]{4,3,2,1,0:T(8,128)S(1)}, u32[]{:S(2)}, u32[]{:S(2)}) collective-permute-start(f32[1,1,1,8,128]{4,3,2,1,0:T(8,128)S(1)} %get-tuple-element.14), channel_id=1, source_target_pairs={{4,0},{8,4},{12,8},{0,12},{5,1},{9,5},{13,9},{1,13},{6,2},{10,6},{... | collective-permute-start | bytes 12296 | tf_op jit(solution)/shard_map/ppermute | solution.py:13
  667.9 8.0 %collective-permute-start.82 = (f32[1,1,1,8,128]{4,3,2,1,0:T(8,128)S(1)}, f32[1,1,1,8,128]{4,3,2,1,0:T(8,128)S(1)}, u32[]{:S(2)}, u32[]{:S(2)}) collective-permute-start(f32[1,1,1,8,128]{4,3,2,1,0:T(8,128)S(1)} %get-tuple-element.13), channel_id=1, source_target_pairs={{3,0},{0,1},{1,2},{2,3},{7,4},{4,5},{5,6},{6,7},{11,8},{8,9},{9,10... | collective-permute-start | bytes 12296 | tf_op jit(solution)/shard_map/ppermute | solution.py:13
  667.9 8.0 %collective-permute-start.83 = (f32[1,1,1,8,128]{4,3,2,1,0:T(8,128)S(1)}, f32[1,1,1,8,128]{4,3,2,1,0:T(8,128)S(1)}, u32[]{:S(2)}, u32[]{:S(2)}) collective-permute-start(f32[1,1,1,8,128]{4,3,2,1,0:T(8,128)S(1)} %get-tuple-element.12), channel_id=1, source_target_pairs={{1,0},{2,1},{3,2},{0,3},{5,4},{6,5},{7,6},{4,7},{9,8},{10,9},{11,1... | collective-permute-start | bytes 12296 | tf_op jit(solution)/shard_map/ppermute | solution.py:13
  718.5 8.1 %collective-permute-start.85 = (f32[1,1,1,8,128]{4,3,2,1,0:T(8,128)S(1)}, f32[1,1,1,8,128]{4,3,2,1,0:T(8,128)S(1)}, u32[]{:S(2)}, u32[]{:S(2)}) collective-permute-start(f32[1,1,1,8,128]{4,3,2,1,0:T(8,128)S(1)} %get-tuple-element.58), channel_id=1, source_target_pairs={{16,0},{0,16},{17,1},{1,17},{18,2},{2,18},{19,3},{3,19},{20,4},{4,... | collective-permute-start | bytes 12296 | tf_op jit(solution)/shard_map/ppermute | solution.py:13
  719.0 7.6 collective-permute-start.86
  738.7 7.3 collective-permute-start.91
  (68 other events, 757.5 us)
where the time goes:
time: 789 us; the launch traced here: 788 us
  blocking collectives  555 us (70%)
  starting transfers between devices  131 us (17%)
  matrix products  43.7 us (6%)
  waiting for transfers between devices  36.2 us (5%)
  local copies, waits for them, and re-layouts  12.5 us (2%)
    all_gather x4, blocking collectives, coarse_weights(): lax.all_gather(on_modes, ('gx', 'gy', 'gz'), axis=0, tiled=True)  268 us
    psum x4, blocking collectives, energy_sum(): lax.psum(partial_inner(first, second), ('gx', 'gy', 'gz')).reshape(-1, 1, 1)  169 us
    ppermute x96, starting transfers between devices, from_behind(): return lax.ppermute(block, axis, route)  131 us
    psum x3, blocking collectives, on_device(): lax.psum(partial_inner(direction, dual_image), ('gx', 'gy', 'gz'))  118 us
    dot_general x4, matrix products, on_device(): jnp.dot(local_flattened, matrix, precision=highest)  40.3 us
    ppermute x96, waiting for transfers between devices, from_behind(): return lax.ppermute(block, axis, route)  36.2 us
  transfers between devices with their start and end apart: 96, of which 24 were waited for; matrix products, arithmetic and copies ran while one was open for 1% of the time, Pallas kernels for 0%

commit v1 on v0

--- a/solution.py
+++ b/solution.py
@@ -5,6 +5,28 @@
 
 ITERS = 4
 highest = lax.Precision.HIGHEST
+
+
+def laid_out(parts, dim):
+    parts = jnp.moveaxis(parts, 0, dim)
+    dims = parts.shape
+    return parts.reshape(*dims[:dim], dims[dim] * dims[dim + 1], *dims[dim + 2 :])
+
+
+def doubled(shard, axis):
+    size = lax.axis_size(axis)
+    blocks = shard[None]
+    for level in range(size.bit_length() - 1):
+        bit = 1 << level
+        other = lax.ppermute(blocks, axis, [(i, i ^ bit) for i in range(size)])
+        both = jnp.stack([blocks, other])
+        upper = lax.axis_index(axis) >> level & 1
+        blocks = jnp.where(upper == 0, both, both[::-1]).reshape(-1, *shard.shape)
+    return blocks
+
+
+def gather_by_bits(x, axis, dim):
+    return laid_out(doubled(x, axis), dim)
 
 
 def from_behind(block, axis, distance):
@@ -52,11 +74,7 @@
 
 def coarse_weights(flattened, own_modes, coarse_rows):
     on_modes = jnp.einsum("jm,km->jk", own_modes, flattened, precision=highest)
-    return jnp.dot(
-        coarse_rows,
-        lax.all_gather(on_modes, ("gx", "gy", "gz"), axis=0, tiled=True),
-        precision=highest,
-    )
+    return jnp.dot(coarse_rows, gather_by_bits(on_modes, ("gx", "gy", "gz"), 0), precision=highest)
 
 
 def on_device(dual_matrix, modes, coarse_rows, loads, face_counts, contact):

time: 789 us -> 559 us (0.71)
  blocking collectives: 555 us -> 276 us
  waiting for transfers between devices: 36.2 us -> 65.5 us
  starting transfers between devices: 131 us -> 148 us
    all_gather x4 -> x0, blocking collectives: 268 us -> none  [coarse_weights(): lax.all_gather(on_modes, ('gx', 'gy', 'gz'), axis=0, tiled=True)]
    ppermute x0 -> x20, waiting for transfers between devices: none -> 40.1 us  [doubled(): other = lax.ppermute(blocks, axis, [(i, i ^ bit) for i in range(size)])]
    ppermute x0 -> x20, starting transfers between devices: none -> 27.1 us  [doubled(): other = lax.ppermute(blocks, axis, [(i, i ^ bit) for i in range(size)])]
    psum x4, blocking collectives: 169 us -> 158 us  [energy_sum(): lax.psum(partial_inner(first, second), ('gx', 'gy', 'gz')).reshape(-1, 1, 1)]
    ppermute x96, waiting for transfers between devices: 36.2 us -> 25.4 us  [from_behind(): return lax.ppermute(block, axis, route)]
    ppermute x96, starting transfers between devices: 131 us -> 121 us  [from_behind(): return lax.ppermute(block, axis, route)]
  transfers between devices with their start and end apart: 96 -> 116, of which waited for: 24 -> 39; matrix products, arithmetic and copies ran while one was open for 1% -> 2% of each run, Pallas kernels for 0% -> 0%
where the time goes in v1:
time: 559 us; the launch traced here: 558 us
  blocking collectives  276 us (49%)
  starting transfers between devices  148 us (26%)
  waiting for transfers between devices  65.5 us (12%)
  matrix products  43 us (8%)
  local copies, waits for them, and re-layouts  14.8 us (3%)
  other arithmetic  7.95 us (1%)
    psum x4, blocking collectives, energy_sum(): lax.psum(partial_inner(first, second), ('gx', 'gy', 'gz')).reshape(-1, 1, 1)  158 us
    ppermute x96, starting transfers between devices, from_behind(): return lax.ppermute(block, axis, route)  121 us
    psum x3, blocking collectives, on_device(): lax.psum(partial_inner(direction, dual_image), ('gx', 'gy', 'gz'))  118 us
    dot_general x4, matrix products, on_device(): jnp.dot(local_flattened, matrix, precision=highest)  40.3 us
    ppermute x20, waiting for transfers between devices, doubled(): other = lax.ppermute(blocks, axis, [(i, i ^ bit) for i in range(size)])  40.1 us
    ppermute x20, starting transfers between devices, doubled(): other = lax.ppermute(blocks, axis, [(i, i ^ bit) for i in range(size)])  27.1 us
    ppermute x96, waiting for transfers between devices, from_behind(): return lax.ppermute(block, axis, route)  25.4 us
  transfers between devices with their start and end apart: 116, of which 39 were waited for; matrix products, arithmetic and copies ran while one was open for 2% of the time, Pallas kernels for 0%

profile of v1, /device:TPU:0, one launch (start us, length us, event | category | flops | bytes accessed | tf_op | source)
XLA Modules:
  0.0 557.6 jit_solution(4386805252269204090)
XLA Ops:
  7.3 2.9 collective-permute-start.2
  21.6 2.7 collective-permute-start.7
  27.0 2.9 collective-permute-done.8
  41.0 2.3 collective-permute-start.16
  45.7 9.7 %copy.123 = f32[1,1,1,1536,1536]{3,4,2,1,0:T(8,128)} copy(f32[1,1,1,1536,1536]{4,3,2,1,0:T(8,128)} %param.6) | data formatting | bytes 18874368 | tf_op args[0]
  56.1 2.7 collective-permute-start.20
  60.2 2.5 collective-permute-start.22
  64.2 10.1 %convolution_bitcast_fusion.6 = f32[1,1,1,8,6,256]{5,3,4,2,1,0:T(8,128)S(1)} fusion(f32[8,1536,1]{1,0,2:T(8,128)S(1)} %bitcast.1178, f32[6,256,1536]{2,1,0:T(8,128)} %bitcast.1162), kind=kOutput, calls=%fused_computation.6 | convolution fusion | flops 226492416 | bytes 9535488 | tf_op jit(solution)/shard_map/dot_general | solution.py:141
  75.2 2.7 collective-permute-start.26
  79.1 2.5 collective-permute-start.28
  83.4 39.5 %all-reduce = (f32[8]{0:T(128)S(1)}, f32[8]{0:T(128)S(1)}) all-reduce(f32[8]{0:T(128)S(1)} %get-tuple-element.3, f32[8]{0:T(128)S(1)} %get-tuple-element.2), channel_id=1, replica_groups=mesh['gx'=2,'gy'=4,'gz'=4] {'gx','gy','gz'}, use_global_device_ids=true, to_apply=%region_1.2 | all-reduce | flops 16 | bytes 128 | tf_op jit(solution)/shard_map/psum | solution.py:131
  136.4 2.4 collective-permute-start.36
  142.0 2.7 collective-permute-done.37
  155.7 2.4 collective-permute-start.45
  159.8 39.5 %psum.58 = f32[8]{0:T(128)S(1)} all-reduce(f32[8]{0:T(128)S(1)} %multiply_reduce_fusion.5), channel_id=1, replica_groups=mesh['gx'=2,'gy'=4,'gz'=4] {'gx','gy','gz'}, use_global_device_ids=true, to_apply=%region_5.6 | all-reduce | flops 8 | bytes 64 | tf_op jit(solution)/shard_map/psum | solution.py:131
  208.9 10.1 %convolution_bitcast_fusion.4 = f32[1,1,1,8,6,256]{5,3,4,2,1,0:T(8,128)S(1)} fusion(f32[8,1536,1]{1,0,2:T(8,128)S(1)} %bitcast.1179, f32[6,256,1536]{2,1,0:T(8,128)} %bitcast.1163), kind=kOutput, calls=%fused_computation.4 | convolution fusion | flops 226492416 | bytes 9535488 | tf_op jit(solution)/shard_map/dot_general | solution.py:141
  223.9 2.5 collective-permute-start.57
  228.1 39.3 %psum.59 = f32[8]{0:T(128)S(1)} all-reduce(f32[8]{0:T(128)S(1)} %multiply_reduce_fusion.4), channel_id=1, replica_groups=mesh['gx'=2,'gy'=4,'gz'=4] {'gx','gy','gz'}, use_global_device_ids=true, to_apply=%region_7.8 | all-reduce | flops 8 | bytes 64 | tf_op jit(solution)/shard_map/psum | solution.py:145
  280.9 2.4 collective-permute-start.65
  286.6 2.7 collective-permute-done.66
  300.3 2.4 collective-permute-start.74
  304.4 39.6 %psum.60 = f32[8]{0:T(128)S(1)} all-reduce(f32[8]{0:T(128)S(1)} %multiply_reduce_fusion.3), channel_id=1, replica_groups=mesh['gx'=2,'gy'=4,'gz'=4] {'gx','gy','gz'}, use_global_device_ids=true, to_apply=%region_9.10 | all-reduce | flops 8 | bytes 64 | tf_op jit(solution)/shard_map/psum | solution.py:131
  353.5 10.1 %convolution_bitcast_fusion.2 = f32[1,1,1,8,6,256]{5,3,4,2,1,0:T(8,128)S(1)} fusion(f32[8,1536,1]{1,0,2:T(8,128)S(1)} %bitcast.1180, f32[6,256,1536]{2,1,0:T(8,128)} %bitcast.1164), kind=kOutput, calls=%fused_computation.2 | convolution fusion | flops 226492416 | bytes 9535488 | tf_op jit(solution)/shard_map/dot_general | solution.py:141
  368.5 2.5 collective-permute-start.86
  372.7 39.6 %psum.61 = f32[8]{0:T(128)S(1)} all-reduce(f32[8]{0:T(128)S(1)} %multiply_reduce_fusion.2), channel_id=1, replica_groups=mesh['gx'=2,'gy'=4,'gz'=4] {'gx','gy','gz'}, use_global_device_ids=true, to_apply=%region_11.12 | all-reduce | flops 8 | bytes 64 | tf_op jit(solution)/shard_map/psum | solution.py:145
  425.8 2.4 collective-permute-start.94
  431.4 2.7 collective-permute-done.95
  445.1 2.4 collective-permute-start.103
  449.2 39.5 %psum.62 = f32[8]{0:T(128)S(1)} all-reduce(f32[8]{0:T(128)S(1)} %multiply_reduce_fusion.1), channel_id=1, replica_groups=mesh['gx'=2,'gy'=4,'gz'=4] {'gx','gy','gz'}, use_global_device_ids=true, to_apply=%region_13.14 | all-reduce | flops 8 | bytes 64 | tf_op jit(solution)/shard_map/psum | solution.py:131
  498.3 10.1 %convolution_bitcast_fusion = f32[1,1,1,8,6,256]{5,3,4,2,1,0:T(8,128)S(1)} fusion(f32[8,1536,1]{1,0,2:T(8,128)S(1)} %bitcast.1181, f32[6,256,1536]{2,1,0:T(8,128)} %bitcast.1165), kind=kOutput, calls=%fused_computation | convolution fusion | flops 226492416 | bytes 9535488 | tf_op jit(solution)/shard_map/dot_general | solution.py:141
  513.4 2.5 collective-permute-start.115
  517.6 39.3 %psum.63 = f32[8]{0:T(128)S(1)} all-reduce(f32[8]{0:T(128)S(1)} %multiply_reduce_fusion), channel_id=1, replica_groups=mesh['gx'=2,'gy'=4,'gz'=4] {'gx','gy','gz'}, use_global_device_ids=true, to_apply=%region_15.16 | all-reduce | flops 8 | bytes 64 | tf_op jit(solution)/shard_map/psum | solution.py:145
  (452 shorter events, 178.2 us)
Async XLA Ops:
  7.2 8.0 %collective-permute-start.1 = (f32[1,1,1,8,128]{4,3,2,1,0:T(8,128)S(1)}, f32[1,1,1,8,128]{4,3,2,1,0:T(8,128)S(1)}, u32[]{:S(2)}, u32[]{:S(2)}) collective-permute-start(f32[1,1,1,8,128]{4,3,2,1,0:T(8,128)S(1)} %get-tuple-element.100), channel_id=1, source_target_pairs={{16,0},{0,16},{17,1},{1,17},{18,2},{2,18},{19,3},{3,19},{20,4},{4,... | collective-permute-start | bytes 12296 | tf_op jit(solution)/shard_map/ppermute | solution.py:35
  7.3 8.0 %collective-permute-start.2 = (f32[1,1,1,8,128]{4,3,2,1,0:T(8,128)S(1)}, f32[1,1,1,8,128]{4,3,2,1,0:T(8,128)S(1)}, u32[]{:S(2)}, u32[]{:S(2)}) collective-permute-start(f32[1,1,1,8,128]{4,3,2,1,0:T(8,128)S(1)} %get-tuple-element.99), channel_id=1, source_target_pairs={{12,0},{0,4},{4,8},{8,12},{13,1},{1,5},{5,9},{9,13},{14,2},{2,6},{... | collective-permute-start | bytes 12296 | tf_op jit(solution)/shard_map/ppermute | solution.py:35
  36.2 7.1 %collective-permute-start.12 = (f32[1,1,1,8,128]{4,3,2,1,0:T(8,128)S(1)}, f32[1,1,1,8,128]{4,3,2,1,0:T(8,128)S(1)}, u32[]{:S(2)}, u32[]{:S(2)}) collective-permute-start(f32[1,1,1,8,128]{4,3,2,1,0:T(8,128)S(1)} %get-tuple-element.52), channel_id=1, source_target_pairs={{16,0},{0,16},{17,1},{1,17},{18,2},{2,18},{19,3},{3,19},{20,4},{4,... | collective-permute-start | bytes 12296 | tf_op jit(solution)/shard_map/ppermute | solution.py:35
  36.5 6.8 %collective-permute-start.13 = (f32[1,1,1,8,128]{4,3,2,1,0:T(8,128)S(1)}, f32[1,1,1,8,128]{4,3,2,1,0:T(8,128)S(1)}, u32[]{:S(2)}, u32[]{:S(2)}) collective-permute-start(f32[1,1,1,8,128]{4,3,2,1,0:T(8,128)S(1)} %get-tuple-element.51), channel_id=1, source_target_pairs={{12,0},{0,4},{4,8},{8,12},{13,1},{1,5},{5,9},{9,13},{14,2},{2,6},{... | collective-permute-start | bytes 12296 | tf_op jit(solution)/shard_map/ppermute | solution.py:35
  45.6 14.5 %collective-permute-start.17 = (f32[1,1,1,8,128]{4,3,2,1,0:T(8,128)S(1)}, f32[1,1,1,8,128]{4,3,2,1,0:T(8,128)S(1)}, u32[]{:S(2)}, u32[]{:S(2)}) collective-permute-start(f32[1,1,1,8,128]{4,3,2,1,0:T(8,128)S(1)} %get-tuple-element.95), channel_id=1, source_target_pairs={{16,0},{0,16},{17,1},{1,17},{18,2},{2,18},{19,3},{3,19},{20,4},{4,... | collective-permute-start | bytes 12296 | tf_op jit(solution)/shard_map/ppermute | solution.py:35
  55.4 7.3 %collective-permute-start.18 = (f32[1,1,1,8,128]{4,3,2,1,0:T(8,128)S(1)}, f32[1,1,1,8,128]{4,3,2,1,0:T(8,128)S(1)}, u32[]{:S(2)}, u32[]{:S(2)}) collective-permute-start(f32[1,1,1,8,128]{4,3,2,1,0:T(8,128)S(1)} %get-tuple-element.94), channel_id=1, source_target_pairs={{16,0},{0,16},{17,1},{1,17},{18,2},{2,18},{19,3},{3,19},{20,4},{4,... | collective-permute-start | bytes 12296 | tf_op jit(solution)/shard_map/ppermute | solution.py:35
  55.9 6.8 %collective-permute-start.19 = (f32[1,1,1,8,128]{4,3,2,1,0:T(8,128)S(1)}, f32[1,1,1,8,128]{4,3,2,1,0:T(8,128)S(1)}, u32[]{:S(2)}, u32[]{:S(2)}) collective-permute-start(f32[1,1,1,8,128]{4,3,2,1,0:T(8,128)S(1)} %get-tuple-element.93), channel_id=1, source_target_pairs={{12,0},{0,4},{4,8},{8,12},{13,1},{1,5},{5,9},{9,13},{14,2},{2,6},{... | collective-permute-start | bytes 12296 | tf_op jit(solution)/shard_map/ppermute | solution.py:35
  74.4 7.3 %collective-permute-start.24 = (f32[1,1,1,8,128]{4,3,2,1,0:T(8,128)S(1)}, f32[1,1,1,8,128]{4,3,2,1,0:T(8,128)S(1)}, u32[]{:S(2)}, u32[]{:S(2)}) collective-permute-start(f32[1,1,1,8,128]{4,3,2,1,0:T(8,128)S(1)} %get-tuple-element.46), channel_id=1, source_target_pairs={{16,0},{0,16},{17,1},{1,17},{18,2},{2,18},{19,3},{3,19},{20,4},{4,... | collective-permute-start | bytes 12296 | tf_op jit(solution)/shard_map/ppermute | solution.py:35
  74.9 6.8 %collective-permute-start.25 = (f32[1,1,1,8,128]{4,3,2,1,0:T(8,128)S(1)}, f32[1,1,1,8,128]{4,3,2,1,0:T(8,128)S(1)}, u32[]{:S(2)}, u32[]{:S(2)}) collective-permute-start(f32[1,1,1,8,128]{4,3,2,1,0:T(8,128)S(1)} %get-tuple-element.45), channel_id=1, source_target_pairs={{12,0},{0,4},{4,8},{8,12},{13,1},{1,5},{5,9},{9,13},{14,2},{2,6},{... | collective-permute-start | bytes 12296 | tf_op jit(solution)/shard_map/ppermute | solution.py:35
  123.0 7.8 %collective-permute-start.30 = (f32[1,1,1,8,128]{4,3,2,1,0:T(8,128)S(1)}, f32[1,1,1,8,128]{4,3,2,1,0:T(8,128)S(1)}, u32[]{:S(2)}, u32[]{:S(2)}) collective-permute-start(f32[1,1,1,8,128]{4,3,2,1,0:T(8,128)S(1)} %get-tuple-element.88), channel_id=1, source_target_pairs={{16,0},{0,16},{17,1},{1,17},{18,2},{2,18},{19,3},{3,19},{20,4},{4,... | collective-permute-start | bytes 12296 | tf_op jit(solution)/shard_map/ppermute | solution.py:35
  123.5 7.3 %collective-permute-start.31 = (f32[1,1,1,8,128]{4,3,2,1,0:T(8,128)S(1)}, f32[1,1,1,8,128]{4,3,2,1,0:T(8,128)S(1)}, u32[]{:S(2)}, u32[]{:S(2)}) collective-permute-start(f32[1,1,1,8,128]{4,3,2,1,0:T(8,128)S(1)} %get-tuple-element.87), channel_id=1, source_target_pairs={{12,0},{0,4},{4,8},{8,12},{13,1},{1,5},{5,9},{9,13},{14,2},{2,6},{... | collective-permute-start | bytes 12296 | tf_op jit(solution)/shard_map/ppermute | solution.py:35
  151.0 7.1 %collective-permute-start.41 = (f32[1,1,1,8,128]{4,3,2,1,0:T(8,128)S(1)}, f32[1,1,1,8,128]{4,3,2,1,0:T(8,128)S(1)}, u32[]{:S(2)}, u32[]{:S(2)}) collective-permute-start(f32[1,1,1,8,128]{4,3,2,1,0:T(8,128)S(1)} %get-tuple-element.40), channel_id=1, source_target_pairs={{16,0},{0,16},{17,1},{1,17},{18,2},{2,18},{19,3},{3,19},{20,4},{4,... | collective-permute-start | bytes 12296 | tf_op jit(solution)/shard_map/ppermute | solution.py:35
  151.3 6.8 %collective-permute-start.42 = (f32[1,1,1,8,128]{4,3,2,1,0:T(8,128)S(1)}, f32[1,1,1,8,128]{4,3,2,1,0:T(8,128)S(1)}, u32[]{:S(2)}, u32[]{:S(2)}) collective-permute-start(f32[1,1,1,8,128]{4,3,2,1,0:T(8,128)S(1)} %get-tuple-element.39), channel_id=1, source_target_pairs={{12,0},{0,4},{4,8},{8,12},{13,1},{1,5},{5,9},{9,13},{14,2},{2,6},{... | collective-permute-start | bytes 12296 | tf_op jit(solution)/shard_map/ppermute | solution.py:35
  199.5 7.7 %collective-permute-start.47 = (f32[1,1,1,8,128]{4,3,2,1,0:T(8,128)S(1)}, f32[1,1,1,8,128]{4,3,2,1,0:T(8,128)S(1)}, u32[]{:S(2)}, u32[]{:S(2)}) collective-permute-start(f32[1,1,1,8,128]{4,3,2,1,0:T(8,128)S(1)} %get-tuple-element.82), channel_id=1, source_target_pairs={{16,0},{0,16},{17,1},{1,17},{18,2},{2,18},{19,3},{3,19},{20,4},{4,... | collective-permute-start | bytes 12296 | tf_op jit(solution)/shard_map/ppermute | solution.py:35
  199.9 7.2 %collective-permute-start.48 = (f32[1,1,1,8,128]{4,3,2,1,0:T(8,128)S(1)}, f32[1,1,1,8,128]{4,3,2,1,0:T(8,128)S(1)}, u32[]{:S(2)}, u32[]{:S(2)}) collective-permute-start(f32[1,1,1,8,128]{4,3,2,1,0:T(8,128)S(1)} %get-tuple-element.81), channel_id=1, source_target_pairs={{12,0},{0,4},{4,8},{8,12},{13,1},{1,5},{5,9},{9,13},{14,2},{2,6},{... | collective-permute-start | bytes 12296 | tf_op jit(solution)/shard_map/ppermute | solution.py:35
  219.1 7.3 %collective-permute-start.53 = (f32[1,1,1,8,128]{4,3,2,1,0:T(8,128)S(1)}, f32[1,1,1,8,128]{4,3,2,1,0:T(8,128)S(1)}, u32[]{:S(2)}, u32[]{:S(2)}) collective-permute-start(f32[1,1,1,8,128]{4,3,2,1,0:T(8,128)S(1)} %get-tuple-element.34), channel_id=1, source_target_pairs={{16,0},{0,16},{17,1},{1,17},{18,2},{2,18},{19,3},{3,19},{20,4},{4,... | collective-permute-start | bytes 12296 | tf_op jit(solution)/shard_map/ppermute | solution.py:35
  219.6 6.8 %collective-permute-start.54 = (f32[1,1,1,8,128]{4,3,2,1,0:T(8,128)S(1)}, f32[1,1,1,8,128]{4,3,2,1,0:T(8,128)S(1)}, u32[]{:S(2)}, u32[]{:S(2)}) collective-permute-start(f32[1,1,1,8,128]{4,3,2,1,0:T(8,128)S(1)} %get-tuple-element.33), channel_id=1, source_target_pairs={{12,0},{0,4},{4,8},{8,12},{13,1},{1,5},{5,9},{9,13},{14,2},{2,6},{... | collective-permute-start | bytes 12296 | tf_op jit(solution)/shard_map/ppermute | solution.py:35
  267.5 7.8 %collective-permute-start.59 = (f32[1,1,1,8,128]{4,3,2,1,0:T(8,128)S(1)}, f32[1,1,1,8,128]{4,3,2,1,0:T(8,128)S(1)}, u32[]{:S(2)}, u32[]{:S(2)}) collective-permute-start(f32[1,1,1,8,128]{4,3,2,1,0:T(8,128)S(1)} %get-tuple-element.76), channel_id=1, source_target_pairs={{16,0},{0,16},{17,1},{1,17},{18,2},{2,18},{19,3},{3,19},{20,4},{4,... | collective-permute-start | bytes 12296 | tf_op jit(solution)/shard_map/ppermute | solution.py:35
  268.0 7.4 %collective-permute-start.60 = (f32[1,1,1,8,128]{4,3,2,1,0:T(8,128)S(1)}, f32[1,1,1,8,128]{4,3,2,1,0:T(8,128)S(1)}, u32[]{:S(2)}, u32[]{:S(2)}) collective-permute-start(f32[1,1,1,8,128]{4,3,2,1,0:T(8,128)S(1)} %get-tuple-element.75), channel_id=1, source_target_pairs={{12,0},{0,4},{4,8},{8,12},{13,1},{1,5},{5,9},{9,13},{14,2},{2,6},{... | collective-permute-start | bytes 12296 | tf_op jit(solution)/shard_map/ppermute | solution.py:35
  295.6 7.1 %collective-permute-start.70 = (f32[1,1,1,8,128]{4,3,2,1,0:T(8,128)S(1)}, f32[1,1,1,8,128]{4,3,2,1,0:T(8,128)S(1)}, u32[]{:S(2)}, u32[]{:S(2)}) collective-permute-start(f32[1,1,1,8,128]{4,3,2,1,0:T(8,128)S(1)} %get-tuple-element.28), channel_id=1, source_target_pairs={{16,0},{0,16},{17,1},{1,17},{18,2},{2,18},{19,3},{3,19},{20,4},{4,... | collective-permute-start | bytes 12296 | tf_op jit(solution)/shard_map/ppermute | solution.py:35
  295.9 6.8 %collective-permute-start.71 = (f32[1,1,1,8,128]{4,3,2,1,0:T(8,128)S(1)}, f32[1,1,1,8,128]{4,3,2,1,0:T(8,128)S(1)}, u32[]{:S(2)}, u32[]{:S(2)}) collective-permute-start(f32[1,1,1,8,128]{4,3,2,1,0:T(8,128)S(1)} %get-tuple-element.27), channel_id=1, source_target_pairs={{12,0},{0,4},{4,8},{8,12},{13,1},{1,5},{5,9},{9,13},{14,2},{2,6},{... | collective-permute-start | bytes 12296 | tf_op jit(solution)/shard_map/ppermute | solution.py:35
  344.0 7.7 %collective-permute-start.76 = (f32[1,1,1,8,128]{4,3,2,1,0:T(8,128)S(1)}, f32[1,1,1,8,128]{4,3,2,1,0:T(8,128)S(1)}, u32[]{:S(2)}, u32[]{:S(2)}) collective-permute-start(f32[1,1,1,8,128]{4,3,2,1,0:T(8,128)S(1)} %get-tuple-element.70), channel_id=1, source_target_pairs={{16,0},{0,16},{17,1},{1,17},{18,2},{2,18},{19,3},{3,19},{20,4},{4,... | collective-permute-start | bytes 12296 | tf_op jit(solution)/shard_map/ppermute | solution.py:35
  344.5 7.2 %collective-permute-start.77 = (f32[1,1,1,8,128]{4,3,2,1,0:T(8,128)S(1)}, f32[1,1,1,8,128]{4,3,2,1,0:T(8,128)S(1)}, u32[]{:S(2)}, u32[]{:S(2)}) collective-permute-start(f32[1,1,1,8,128]{4,3,2,1,0:T(8,128)S(1)} %get-tuple-element.69), channel_id=1, source_target_pairs={{12,0},{0,4},{4,8},{8,12},{13,1},{1,5},{5,9},{9,13},{14,2},{2,6},{... | collective-permute-start | bytes 12296 | tf_op jit(solution)/shard_map/ppermute | solution.py:35
  363.7 7.3 %collective-permute-start.82 = (f32[1,1,1,8,128]{4,3,2,1,0:T(8,128)S(1)}, f32[1,1,1,8,128]{4,3,2,1,0:T(8,128)S(1)}, u32[]{:S(2)}, u32[]{:S(2)}) collective-permute-start(f32[1,1,1,8,128]{4,3,2,1,0:T(8,128)S(1)} %get-tuple-element.22), channel_id=1, source_target_pairs={{16,0},{0,16},{17,1},{1,17},{18,2},{2,18},{19,3},{3,19},{20,4},{4,... | collective-permute-start | bytes 12296 | tf_op jit(solution)/shard_map/ppermute | solution.py:35
  364.2 6.8 %collective-permute-start.83 = (f32[1,1,1,8,128]{4,3,2,1,0:T(8,128)S(1)}, f32[1,1,1,8,128]{4,3,2,1,0:T(8,128)S(1)}, u32[]{:S(2)}, u32[]{:S(2)}) collective-permute-start(f32[1,1,1,8,128]{4,3,2,1,0:T(8,128)S(1)} %get-tuple-element.21), channel_id=1, source_target_pairs={{12,0},{0,4},{4,8},{8,12},{13,1},{1,5},{5,9},{9,13},{14,2},{2,6},{... | collective-permute-start | bytes 12296 | tf_op jit(solution)/shard_map/ppermute | solution.py:35
  412.4 7.9 %collective-permute-start.88 = (f32[1,1,1,8,128]{4,3,2,1,0:T(8,128)S(1)}, f32[1,1,1,8,128]{4,3,2,1,0:T(8,128)S(1)}, u32[]{:S(2)}, u32[]{:S(2)}) collective-permute-start(f32[1,1,1,8,128]{4,3,2,1,0:T(8,128)S(1)} %get-tuple-element.64), channel_id=1, source_target_pairs={{16,0},{0,16},{17,1},{1,17},{18,2},{2,18},{19,3},{3,19},{20,4},{4,... | collective-permute-start | bytes 12296 | tf_op jit(solution)/shard_map/ppermute | solution.py:35
  412.9 7.4 %collective-permute-start.89 = (f32[1,1,1,8,128]{4,3,2,1,0:T(8,128)S(1)}, f32[1,1,1,8,128]{4,3,2,1,0:T(8,128)S(1)}, u32[]{:S(2)}, u32[]{:S(2)}) collective-permute-start(f32[1,1,1,8,128]{4,3,2,1,0:T(8,128)S(1)} %get-tuple-element.63), channel_id=1, source_target_pairs={{12,0},{0,4},{4,8},{8,12},{13,1},{1,5},{5,9},{9,13},{14,2},{2,6},{... | collective-permute-start | bytes 12296 | tf_op jit(solution)/shard_map/ppermute | solution.py:35
  440.4 7.1 %collective-permute-start.99 = (f32[1,1,1,8,128]{4,3,2,1,0:T(8,128)S(1)}, f32[1,1,1,8,128]{4,3,2,1,0:T(8,128)S(1)}, u32[]{:S(2)}, u32[]{:S(2)}) collective-permute-start(f32[1,1,1,8,128]{4,3,2,1,0:T(8,128)S(1)} %get-tuple-element.16), channel_id=1, source_target_pairs={{16,0},{0,16},{17,1},{1,17},{18,2},{2,18},{19,3},{3,19},{20,4},{4,... | collective-permute-start | bytes 12296 | tf_op jit(solution)/shard_map/ppermute | solution.py:35
  440.7 6.8 %collective-permute-start.100 = (f32[1,1,1,8,128]{4,3,2,1,0:T(8,128)S(1)}, f32[1,1,1,8,128]{4,3,2,1,0:T(8,128)S(1)}, u32[]{:S(2)}, u32[]{:S(2)}) collective-permute-start(f32[1,1,1,8,128]{4,3,2,1,0:T(8,128)S(1)} %get-tuple-element.15), channel_id=1, source_target_pairs={{12,0},{0,4},{4,8},{8,12},{13,1},{1,5},{5,9},{9,13},{14,2},{2,6},{... | collective-permute-start | bytes 12296 | tf_op jit(solution)/shard_map/ppermute | solution.py:35
  488.9 7.6 %collective-permute-start.105 = (f32[1,1,1,8,128]{4,3,2,1,0:T(8,128)S(1)}, f32[1,1,1,8,128]{4,3,2,1,0:T(8,128)S(1)}, u32[]{:S(2)}, u32[]{:S(2)}) collective-permute-start(f32[1,1,1,8,128]{4,3,2,1,0:T(8,128)S(1)} %get-tuple-element.58), channel_id=1, source_target_pairs={{16,0},{0,16},{17,1},{1,17},{18,2},{2,18},{19,3},{3,19},{20,4},{4,... | collective-permute-start | bytes 12296 | tf_op jit(solution)/shard_map/ppermute | solution.py:35
  489.4 7.2 %collective-permute-start.106 = (f32[1,1,1,8,128]{4,3,2,1,0:T(8,128)S(1)}, f32[1,1,1,8,128]{4,3,2,1,0:T(8,128)S(1)}, u32[]{:S(2)}, u32[]{:S(2)}) collective-permute-start(f32[1,1,1,8,128]{4,3,2,1,0:T(8,128)S(1)} %get-tuple-element.57), channel_id=1, source_target_pairs={{12,0},{0,4},{4,8},{8,12},{13,1},{1,5},{5,9},{9,13},{14,2},{2,6},{... | collective-permute-start | bytes 12296 | tf_op jit(solution)/shard_map/ppermute | solution.py:35
  508.6 7.3 %collective-permute-start.111 = (f32[1,1,1,8,128]{4,3,2,1,0:T(8,128)S(1)}, f32[1,1,1,8,128]{4,3,2,1,0:T(8,128)S(1)}, u32[]{:S(2)}, u32[]{:S(2)}) collective-permute-start(f32[1,1,1,8,128]{4,3,2,1,0:T(8,128)S(1)} %get-tuple-element.10), channel_id=1, source_target_pairs={{16,0},{0,16},{17,1},{1,17},{18,2},{2,18},{19,3},{3,19},{20,4},{4,... | collective-permute-start | bytes 12296 | tf_op jit(solution)/shard_map/ppermute | solution.py:35
  (88 other events, 689.1 us)
